TPU v7x, 128 devices: a whole 4x4x4 slice. The times are simulated.
128 devices in a mesh: row: 32 (over z, y, core), feat: 4 (over x).
Axes of the slice: x: 4, y: 4, z: 4, core: 2. Of those that a mesh axis runs over, the one named last changes fastest.
Arguments:
- bins: int32 [256, 131072], P('feat', 'row'), may hold values from 0 to 255
- grad: bfloat16 [131072], P('row'), as said below
- hess: bfloat16 [131072], P('row'), may hold values from 0.019897461 to 0.19921875
- margin: float32 [131072], P('row'), may hold values from -6 to 6
- node_start: int32 [131072], P('row'), may hold values from 0 to 7
- split_feat1: int32 [8], replicated, may hold values from 0 to 255
- split_bin1: int32 [8], replicated, may hold values from 0 to 255
- split_feat2: int32 [16], replicated, may hold values from 0 to 255
- split_bin2: int32 [16], replicated, may hold values from 0 to 255
Outputs:
- gain1: float32 [8, 256, 256], P(None, ('feat', 'row'))
- gain2: float32 [16, 256, 256], P(None, ('feat', 'row'))
- new_margin: float32 [131072], P('row')
Inputs may be any that keep to these rules, and one draw needn't show every extreme that they name: `grad`: gradients of one model's loss, one for each row.
All inputs are finite; a program needn't handle non-finite values.
Results may differ from a plain program's by a relative error of at most 0.0003.
Values sent between devices are 32-bit elements; how exact they have to be, the bound alone decides.
A program may use at most 64 MiB of HBM per device.

v0:
```python
import math

import jax
import jax.numpy as jnp
from jax import lax
from jax.sharding import PartitionSpec as P

B = 256
NODES1 = 8
NODES2 = 16
LEAVES = 32


LAMBDA = 1.0
RATE = 0.3


def lookup(table, index):
    slots = jnp.arange(table.shape[0], dtype=jnp.int32)
    zero = jnp.zeros((), table.dtype)
    return jnp.sum(jnp.where(index[:, None] == slots[None, :], table[None, :], zero), axis=1)


def node_weights(grad, hess, node, count, stride):
    slots = jnp.arange(count, dtype=jnp.int32) * stride
    member = node[:, None] == slots[None, :]
    zero = jnp.zeros((), jnp.bfloat16)
    return jnp.concatenate(
        [jnp.where(member, grad[:, None], zero), jnp.where(member, hess[:, None], zero)], axis=1
    )


def hist_term(bins, weights, count):
    width = count // B
    block = math.gcd(width, 8)
    rows = bins.shape[1]
    groups = bins.reshape(width // block, block, rows)
    levels = jnp.arange(B, dtype=jnp.int32)

    def one_group(group):
        table = (group[:, :, None] == levels[None, None, :]).astype(jnp.bfloat16)
        return lax.dot_general(
            table, weights, (((1,), (0,)), ((), ())), preferred_element_type=jnp.float32
        )

    parts = lax.map(one_group, groups)
    return parts.reshape(count, weights.shape[1])


def arrange(owned, nodes):
    per_owner = owned.shape[0] // B
    return owned.reshape(per_owner, B, 2 * nodes).transpose(2, 0, 1).reshape(2, nodes, per_owner, B)


def split_gain(hist):
    summed = jnp.cumsum(hist, axis=-1)
    grad_left = summed[0]
    hess_left = summed[1]
    grad_total = summed[0][..., -1:]
    hess_total = summed[1][..., -1:]
    grad_right = grad_total - grad_left
    hess_right = hess_total - hess_left
    return (
        grad_left * grad_left / (hess_left + LAMBDA)
        + grad_right * grad_right / (hess_right + LAMBDA)
        - grad_total * grad_total / (hess_total + LAMBDA)
    )


def route_part(bins, node, feats, cuts):
    local_count = bins.shape[0]
    base = lax.axis_index("feat") * local_count
    column = lookup(feats, node) - base
    owned = (column >= 0) & (column < local_count)
    picked = jnp.take_along_axis(bins, jnp.clip(column, 0, local_count - 1)[None, :], axis=0)[0]
    right = owned & (picked > lookup(cuts, node))
    return (right, owned)


def body(bins, grad, hess, margin, node_start, split_feat1, split_bin1, split_feat2, split_bin2):
    local_count = bins.shape[0]
    own_rows = local_count * B // lax.axis_size("row")
    first_weights = node_weights(grad, hess, node_start, NODES1, 1)
    hist1 = arrange(
        lax.psum_scatter(
            hist_term(bins, first_weights, own_rows * lax.axis_size("row")),
            "row",
            scatter_dimension=0,
            tiled=True,
        ),
        NODES1,
    )
    gain1 = split_gain(hist1)
    right_part, owned_first = route_part(bins, node_start, split_feat1, split_bin1)
    right_sum = lax.psum(right_part.astype(jnp.float32), "feat")
    child = 2 * node_start + (right_sum > 0.5).astype(jnp.int32)
    second_weights = node_weights(grad, hess, child, NODES2, 1)
    hist2 = arrange(
        lax.psum_scatter(
            hist_term(bins, second_weights, own_rows * lax.axis_size("row")),
            "row",
            scatter_dimension=0,
            tiled=True,
        ),
        NODES2,
    )
    gain2 = split_gain(hist2)
    right_second, owned_second = route_part(bins, child, split_feat2, split_bin2)
    direction = lax.psum(right_second.astype(jnp.float32), "feat")
    leaf = 2 * child + (direction > 0.5).astype(jnp.int32)
    slots = jnp.arange(LEAVES, dtype=jnp.int32)
    member = (leaf[:, None] == slots[None, :]).astype(jnp.bfloat16)
    pairs = jnp.stack([grad, hess], axis=1)
    totals = lax.dot_general(
        member, pairs, (((0,), (0,)), ((), ())), preferred_element_type=jnp.float32
    )
    sums = lax.psum(totals, "row")
    weight = -RATE * sums[:, 0] / (sums[:, 1] + LAMBDA)
    new_margin = margin + lookup(weight, leaf)
    return (gain1, gain2, new_margin)


def solution(mesh):
    return jax.shard_map(
        body,
        mesh=mesh,
        in_specs=(P("feat", "row"), P("row"), P("row"), P("row"), P("row"), P(), P(), P(), P()),
        out_specs=(P(None, ("feat", "row"), None), P(None, ("feat", "row"), None), P("row")),
        check_vma=False,
    )
```

profile of v0, /device:TPU:1, one launch (start us, length us, event | category | flops | bytes accessed | tf_op | source)
XLA Modules:
  0.0 308.1 jit_solution(13935059406323790473)
XLA Ops:
  8.0 60.0 %while.22 = (s32[]{:T(128)}, f32[8,8,256,16]{2,1,0,3:T(8,128)S(1)}, s32[8,8,4096]{2,1,0:T(8,128)}, bf16[4096,16]{0,1:T(8,128)(2,1)S(1)}, s32[]{:T(128)}) while((s32[]{:T(128)}, f32[8,8,256,16]{2,1,0,3:T(8,128)S(1)}, s32[8,8,4096]{2,1,0:T(8,128)}, bf16[4096,16]{0,1:T(8,128)(2,1)S(1)}, s32[]{:T(128)}) %tuple.65), condition=%wide.region_1.2_spmd.clone, body=%wide.region_0.1_spmd.clone.sunk | while | flops 276824064 | bytes 917581 | solution.py:46
  8.9 6.5 %fusion.40 = f32[1,8,256,16]{2,3,1,0:T(8,128)S(1)} fusion(s32[8,4096]{1,0:T(8,128)S(1)} %dynamic-slice_bitcast_fusion.4, bf16[4096,16]{0,1:T(8,128)(2,1)S(1)} %get-tuple-element.186), kind=kOutput, calls=%fused_computation.7.clone.1 | convolution fusion | flops 276824064 | bytes 393216 | tf_op jit(solution)/shard_map/while/body/eval_jaxpr/dot_general | solution.py:42
  16.4 6.5 %fusion.40 = f32[1,8,256,16]{2,3,1,0:T(8,128)S(1)} fusion(s32[8,4096]{1,0:T(8,128)S(1)} %dynamic-slice_bitcast_fusion.4, bf16[4096,16]{0,1:T(8,128)(2,1)S(1)} %get-tuple-element.186), kind=kOutput, calls=%fused_computation.7.clone.1 | convolution fusion | flops 276824064 | bytes 393216 | tf_op jit(solution)/shard_map/while/body/eval_jaxpr/dot_general | solution.py:42
  24.0 6.5 %fusion.40 = f32[1,8,256,16]{2,3,1,0:T(8,128)S(1)} fusion(s32[8,4096]{1,0:T(8,128)S(1)} %dynamic-slice_bitcast_fusion.4, bf16[4096,16]{0,1:T(8,128)(2,1)S(1)} %get-tuple-element.186), kind=kOutput, calls=%fused_computation.7.clone.1 | convolution fusion | flops 276824064 | bytes 393216 | tf_op jit(solution)/shard_map/while/body/eval_jaxpr/dot_general | solution.py:42
  31.5 6.5 %fusion.40 = f32[1,8,256,16]{2,3,1,0:T(8,128)S(1)} fusion(s32[8,4096]{1,0:T(8,128)S(1)} %dynamic-slice_bitcast_fusion.4, bf16[4096,16]{0,1:T(8,128)(2,1)S(1)} %get-tuple-element.186), kind=kOutput, calls=%fused_computation.7.clone.1 | convolution fusion | flops 276824064 | bytes 393216 | tf_op jit(solution)/shard_map/while/body/eval_jaxpr/dot_general | solution.py:42
  39.0 6.5 %fusion.40 = f32[1,8,256,16]{2,3,1,0:T(8,128)S(1)} fusion(s32[8,4096]{1,0:T(8,128)S(1)} %dynamic-slice_bitcast_fusion.4, bf16[4096,16]{0,1:T(8,128)(2,1)S(1)} %get-tuple-element.186), kind=kOutput, calls=%fused_computation.7.clone.1 | convolution fusion | flops 276824064 | bytes 393216 | tf_op jit(solution)/shard_map/while/body/eval_jaxpr/dot_general | solution.py:42
  46.5 6.5 %fusion.40 = f32[1,8,256,16]{2,3,1,0:T(8,128)S(1)} fusion(s32[8,4096]{1,0:T(8,128)S(1)} %dynamic-slice_bitcast_fusion.4, bf16[4096,16]{0,1:T(8,128)(2,1)S(1)} %get-tuple-element.186), kind=kOutput, calls=%fused_computation.7.clone.1 | convolution fusion | flops 276824064 | bytes 393216 | tf_op jit(solution)/shard_map/while/body/eval_jaxpr/dot_general | solution.py:42
  54.0 6.5 %fusion.40 = f32[1,8,256,16]{2,3,1,0:T(8,128)S(1)} fusion(s32[8,4096]{1,0:T(8,128)S(1)} %dynamic-slice_bitcast_fusion.4, bf16[4096,16]{0,1:T(8,128)(2,1)S(1)} %get-tuple-element.186), kind=kOutput, calls=%fused_computation.7.clone.1 | convolution fusion | flops 276824064 | bytes 393216 | tf_op jit(solution)/shard_map/while/body/eval_jaxpr/dot_general | solution.py:42
  61.5 6.5 %fusion.40 = f32[1,8,256,16]{2,3,1,0:T(8,128)S(1)} fusion(s32[8,4096]{1,0:T(8,128)S(1)} %dynamic-slice_bitcast_fusion.4, bf16[4096,16]{0,1:T(8,128)(2,1)S(1)} %get-tuple-element.186), kind=kOutput, calls=%fused_computation.7.clone.1 | convolution fusion | flops 276824064 | bytes 393216 | tf_op jit(solution)/shard_map/while/body/eval_jaxpr/dot_general | solution.py:42
  70.2 33.0 %gather_fusion = s32[4096]{0:T(1024)S(1)} fusion(s32[64,4096]{1,0:T(8,128)S(1)} %bitcast.84, s32[4096]{0:T(1024)S(1)} %bitcast.87), kind=kCustom, calls=%fused_computation.clone | custom fusion | bytes 65536 | tf_op jit(solution)/shard_map/jit(take_along_axis)/gather | solution.py:75
  103.3 14.0 %psum.21 = f32[4096]{0:T(1024)S(1)} all-reduce(f32[4096]{0:T(1024)S(1)} %and_convert_fusion.1), channel_id=1, replica_groups=mesh['row'=32,'feat'=4] {'feat'}, use_global_device_ids=true, to_apply=%region_7.9 | all-reduce | flops 4096 | bytes 32768 | tf_op jit(solution)/shard_map/psum | solution.py:95
  117.4 54.9 %while.23 = (s32[]{:T(128)}, f32[8,8,256,32]{2,1,0,3:T(8,128)S(1)}, s32[8,8,4096]{2,1,0:T(8,128)S(1)}, bf16[4096,32]{0,1:T(8,128)(2,1)S(1)}, s32[]{:T(128)}) while((s32[]{:T(128)}, f32[8,8,256,32]{2,1,0,3:T(8,128)S(1)}, s32[8,8,4096]{2,1,0:T(8,128)S(1)}, bf16[4096,32]{0,1:T(8,128)(2,1)S(1)}, s32[]{:T(128)}) %tuple.66), condition=%wide.region_9.11_spmd.clone, body=%wide.region_8.10_spmd.clone.sunk | while | flops 545259520 | bytes 1441869 | solution.py:46
  117.4 6.6 %fusion.42 = f32[1,8,256,32]{2,3,1,0:T(8,128)S(1)} fusion(s32[8,4096]{1,0:T(8,128)S(1)} %dynamic-slice_bitcast_fusion.5, bf16[4096,32]{0,1:T(8,128)(2,1)S(1)} %get-tuple-element.201), kind=kOutput, calls=%fused_computation.14.clone.1 | convolution fusion | flops 545259520 | bytes 655360 | tf_op jit(solution)/shard_map/while/body/eval_jaxpr/dot_general | solution.py:42
  124.3 6.6 %fusion.42 = f32[1,8,256,32]{2,3,1,0:T(8,128)S(1)} fusion(s32[8,4096]{1,0:T(8,128)S(1)} %dynamic-slice_bitcast_fusion.5, bf16[4096,32]{0,1:T(8,128)(2,1)S(1)} %get-tuple-element.201), kind=kOutput, calls=%fused_computation.14.clone.1 | convolution fusion | flops 545259520 | bytes 655360 | tf_op jit(solution)/shard_map/while/body/eval_jaxpr/dot_general | solution.py:42
  131.1 6.6 %fusion.42 = f32[1,8,256,32]{2,3,1,0:T(8,128)S(1)} fusion(s32[8,4096]{1,0:T(8,128)S(1)} %dynamic-slice_bitcast_fusion.5, bf16[4096,32]{0,1:T(8,128)(2,1)S(1)} %get-tuple-element.201), kind=kOutput, calls=%fused_computation.14.clone.1 | convolution fusion | flops 545259520 | bytes 655360 | tf_op jit(solution)/shard_map/while/body/eval_jaxpr/dot_general | solution.py:42
  138.0 6.6 %fusion.42 = f32[1,8,256,32]{2,3,1,0:T(8,128)S(1)} fusion(s32[8,4096]{1,0:T(8,128)S(1)} %dynamic-slice_bitcast_fusion.5, bf16[4096,32]{0,1:T(8,128)(2,1)S(1)} %get-tuple-element.201), kind=kOutput, calls=%fused_computation.14.clone.1 | convolution fusion | flops 545259520 | bytes 655360 | tf_op jit(solution)/shard_map/while/body/eval_jaxpr/dot_general | solution.py:42
  144.8 6.6 %fusion.42 = f32[1,8,256,32]{2,3,1,0:T(8,128)S(1)} fusion(s32[8,4096]{1,0:T(8,128)S(1)} %dynamic-slice_bitcast_fusion.5, bf16[4096,32]{0,1:T(8,128)(2,1)S(1)} %get-tuple-element.201), kind=kOutput, calls=%fused_computation.14.clone.1 | convolution fusion | flops 545259520 | bytes 655360 | tf_op jit(solution)/shard_map/while/body/eval_jaxpr/dot_general | solution.py:42
  151.7 6.6 %fusion.42 = f32[1,8,256,32]{2,3,1,0:T(8,128)S(1)} fusion(s32[8,4096]{1,0:T(8,128)S(1)} %dynamic-slice_bitcast_fusion.5, bf16[4096,32]{0,1:T(8,128)(2,1)S(1)} %get-tuple-element.201), kind=kOutput, calls=%fused_computation.14.clone.1 | convolution fusion | flops 545259520 | bytes 655360 | tf_op jit(solution)/shard_map/while/body/eval_jaxpr/dot_general | solution.py:42
  158.6 6.6 %fusion.42 = f32[1,8,256,32]{2,3,1,0:T(8,128)S(1)} fusion(s32[8,4096]{1,0:T(8,128)S(1)} %dynamic-slice_bitcast_fusion.5, bf16[4096,32]{0,1:T(8,128)(2,1)S(1)} %get-tuple-element.201), kind=kOutput, calls=%fused_computation.14.clone.1 | convolution fusion | flops 545259520 | bytes 655360 | tf_op jit(solution)/shard_map/while/body/eval_jaxpr/dot_general | solution.py:42
  165.4 6.6 %fusion.42 = f32[1,8,256,32]{2,3,1,0:T(8,128)S(1)} fusion(s32[8,4096]{1,0:T(8,128)S(1)} %dynamic-slice_bitcast_fusion.5, bf16[4096,32]{0,1:T(8,128)(2,1)S(1)} %get-tuple-element.201), kind=kOutput, calls=%fused_computation.14.clone.1 | convolution fusion | flops 545259520 | bytes 655360 | tf_op jit(solution)/shard_map/while/body/eval_jaxpr/dot_general | solution.py:42
  172.3 2.6 copy.88
  175.9 33.0 %gather_fusion.1 = s32[4096]{0:T(1024)S(1)} fusion(s32[64,4096]{1,0:T(8,128)S(1)} %bitcast.85, s32[4096]{0:T(1024)S(1)} %bitcast.86), kind=kCustom, calls=%fused_computation.1.clone | custom fusion | bytes 65536 | tf_op jit(solution)/shard_map/jit(take_along_axis)/gather | solution.py:75
  209.0 11.0 %psum.22 = f32[4096]{0:T(1024)S(1)} all-reduce(f32[4096]{0:T(1024)S(1)} %and_convert_fusion), channel_id=1, replica_groups=mesh['row'=32,'feat'=4] {'feat'}, use_global_device_ids=true, to_apply=%region_15.17 | all-reduce | flops 4096 | bytes 32768 | tf_op jit(solution)/shard_map/psum | solution.py:109
  220.3 71.3 %psum.23 = f32[32,2]{0,1:T(2,128)S(1)} all-reduce(f32[32,2]{0,1:T(2,128)S(1)} %fusion.12), channel_id=1, replica_groups=mesh['row'=32,'feat'=4] {'row'}, use_global_device_ids=true, to_apply=%region_16.18 | all-reduce | flops 64 | bytes 512 | tf_op jit(solution)/shard_map/psum | solution.py:117
  (122 shorter events, 23.3 us)
Async XLA Ops:
  7.2 285.1 %reduce-scatter.3.cloned.1.call-start = ((), (), s32[]{:S(2)}) async-start(), calls=%async_computation.2 | async-start | bytes 1081344 | tf_op jit(solution)/shard_map/reduce_scatter | solution.py:85
  68.1 1.7 copy-start.1
  68.1 1.7 copy-start.5
  68.1 1.7 copy-start.6
  68.1 2.0 copy-start
  69.7 227.0 %reduce-scatter.5.cloned.1.call-start = ((), (), s32[]{:S(2)}) async-start(), calls=%async_computation.3 | async-start | bytes 2162688 | tf_op jit(solution)/shard_map/reduce_scatter | solution.py:99
  70.1 47.1 %copy-start.2 = (bf16[4096]{0:T(1024)(128)(2,1)S(1)}, bf16[4096]{0:T(1024)(128)(2,1)}, u32[]{:S(2)}) copy-start(bf16[4096]{0:T(1024)(128)(2,1)} %param.16) | copy-start | bytes 24580
  70.2 47.1 %copy-start.3 = (bf16[4096]{0:T(1024)(128)(2,1)S(1)}, bf16[4096]{0:T(1024)(128)(2,1)}, u32[]{:S(2)}) copy-start(bf16[4096]{0:T(1024)(128)(2,1)} %param.17) | copy-start | bytes 24580
  174.8 0.7 copy-start.7
  174.8 0.7 copy-start.8
  175.9 115.8 %copy-start.4 = (f32[4096]{0:T(1024)S(1)}, f32[4096]{0:T(1024)}, u32[]{:S(2)}) copy-start(f32[4096]{0:T(1024)} %param.18) | copy-start | bytes 49156
Sparse Core Ops, SparseCore 0:
  69.8 79.3 reduce-scatter.2
  175.0 81.3 reduce-scatter.4
where the time goes:
time: 309 us; the launch traced here: 308 us
  matrix products  105 us (34%)
  blocking collectives  96.3 us (31%)
  local copies, waits for them, and re-layouts  84 us (27%)
  between operations  14.5 us (5%)
  other arithmetic  7.57 us (2%)
    dot_general x16, matrix products, one_group(): lax.dot_general(table, weights, (((1,), (0,)), ((), ())), preferred_eleme...  105 us
    psum x1, blocking collectives, body(): sums = lax.psum(totals, 'row')  71.3 us
    gather x2, local copies, waits for them, and re-layouts, route_part(): jnp.take_along_axis(bins, jnp.clip(column, 0, local_count - 1)[None, :],...  66.1 us
    psum x1, blocking collectives, body(): right_sum = lax.psum(right_part.astype(jnp.float32), 'feat')  14 us
    psum x1, blocking collectives, body(): direction = lax.psum(right_second.astype(jnp.float32), 'feat')  11 us
    eq x16, local copies, waits for them, and re-layouts, one_group(): table = (group[:, :, None] == levels[None, None, :]).astype(jnp.bfloat16)  7.46 us
  transfers between devices with their start and end apart: 2, of which 0 were waited for; matrix products, arithmetic and copies ran while one was open for 42% of the time, Pallas kernels for 0%

commit v1 on v0

v1 whole, which is shorter than its diff:
```python
import jax
import jax.numpy as jnp
from jax import lax
from jax.experimental import pallas as pl
from jax.experimental.pallas import tpu as pltpu
from jax.sharding import PartitionSpec as P

B = 256
NODES1 = 8
NODES2 = 16
LAMBDA = 1.0
RATE = 0.3

SEG = 86
HI = 88
LO = 3
COLS = 2 * NODES2
UNROLL = 8

MESH = pl.DeviceIdType.MESH
NT = (((1,), (1,)), ((), ()))
TN = (((0,), (0,)), ((), ()))
f32 = jnp.float32
bf16 = jnp.bfloat16


def iota(shape, dim):
    return lax.broadcasted_iota(jnp.int32, shape, dim)


def kernel(bins, rows, table, out1, out2, out_margin,
           hi_s, lo_s, w_s, picked_s, dir_s, kept, sent, mate, part1, part2, sums, tri,
           x1, x2, leaf_mate, leaf_in, leaf_out,
           x1_ss, x1_rs, x2_ss, x2_rs, core_ss, core_rs, p1_ss, p1_rs, p2_ss, p2_rs, leaf_ss, leaf_rs):
    features, count = bins.shape
    me = lax.axis_index("row")
    feat = lax.axis_index("feat")
    z, y, c = me // 8, (me // 2) % 4, me % 2

    def inner(d):
        return (((z + d * c) % 4) * 8 + ((y + d * (1 - c)) % 4) * 2 + c, feat)

    def outer(d):
        return (((z + d * (1 - c)) % 4) * 8 + ((y + d * c) % 4) * 2 + c, feat)

    sibling = (z * 8 + y * 2 + (1 - c), feat)

    def across(d):
        return (me, (feat + d) % 4)

    peers = [sibling] + [axis(d) for axis in (inner, outer, across) for d in (1, 2, 3)]
    barrier = pltpu.get_barrier_semaphore()
    for peer in peers:
        pl.semaphore_signal(barrier, inc=1, device_id=peer, device_id_type=MESH)

    def remote(src, dst, ss, rs, peer):
        return pltpu.make_async_remote_copy(
            src_ref=src, dst_ref=dst, send_sem=ss, recv_sem=rs, device_id=peer, device_id_type=MESH)

    local = table[:, 0:1] - feat * features
    select = jnp.where(local == iota((32, features), 1), 1.0, 0.0).astype(bf16)
    values = bins[...].astype(f32)
    picked = lax.dot_general(select, values.astype(bf16), (((1,), (0,)), ((), ())), preferred_element_type=f32)
    above = jnp.where(picked > table[:, 1:2].astype(f32), 1.0, 0.0)
    node = rows[2:3, :]
    first = node == iota((NODES1, count), 0).astype(f32)
    x1[3] = jnp.max(jnp.where(first, above[0:8], 0.0), axis=0, keepdims=True)
    picked_s[...] = above[8:24]
    pl.semaphore_wait(barrier, len(peers))
    route1 = [remote(x1.at[3], x1.at[d - 1], x1_ss.at[d - 1], x1_rs.at[d - 1], across(d)) for d in (1, 2, 3)]
    for copy in route1:
        copy.start()

    lo = jnp.where(values >= 2.0 * SEG, 2.0, jnp.where(values >= 1.0 * SEG, 1.0, 0.0))
    lo_s[...] = lo
    hi_s[...] = values - SEG * lo
    h = iota((HI, B), 0)
    for k in range(LO):
        tri[k] = jnp.where((h + k * SEG <= iota((HI, B), 1)) & (h < SEG), 1.0, 0.0).astype(bf16)
    for copy in route1:
        copy.wait_recv()
    right = x1[0] + x1[1] + x1[2] + x1[3]
    child = jnp.where(right > 0.5, 8.0, 0.0) + node
    member = child == iota((NODES2, count), 0).astype(f32)
    dir_s[1] = child
    w_s[0:16, :] = jnp.where(member, rows[0:1, :], 0.0).astype(bf16)
    w_s[16:32, :] = jnp.where(member, rows[1:2, :], 0.0).astype(bf16)
    x2[3] = jnp.max(jnp.where(member, picked_s[...], 0.0), axis=0, keepdims=True)
    route2 = [remote(x2.at[3], x2.at[d - 1], x2_ss.at[d - 1], x2_rs.at[d - 1], across(d)) for d in (1, 2, 3)]
    for copy in route2:
        copy.start()

    def feature(i, j, q):
        zo = (z + 1 + i * (1 - q) + j * q) % 4
        yo = (y + 1 + j * (1 - q) + i * q) % 4
        return zo * 16 + yo * 4 + q * 2

    hi_slots = iota((HI, count), 0).astype(f32).astype(bf16)

    def histogram(f):
        table_hi = jnp.where(hi_s[pl.ds(f, 1), :].astype(bf16) == hi_slots, bf16(1), bf16(0))
        lo_row = jnp.broadcast_to(lo_s[pl.ds(f, 1), :].astype(bf16), (COLS, count))
        weights = w_s[...]
        terms = jnp.concatenate([jnp.where(lo_row == bf16(k), weights, bf16(0)) for k in range(LO)], 0)
        return lax.dot_general(table_hi, terms, NT, preferred_element_type=f32)

    def core_copy(t):
        return remote(sent.at[t], mate.at[t], core_ss.at[t], core_rs.at[t], sibling)

    def p1_copy(i, j):
        return remote(kept.at[i * 4 + j], part1.at[i * 3 + j], p1_ss.at[i * 3 + j], p1_rs.at[i * 3 + j], inner(j + 1))

    def p2_copy(i):
        return remote(kept.at[i * 4 + 3], part2.at[i], p2_ss.at[i], p2_rs.at[i], outer(i + 1))

    def finish(i, j):
        t = i * 4 + j
        core_copy(t).wait_recv()
        kept[t] += mate[t]

    def pass_on(i, j):
        finish(i, j)
        p1_copy(i, j).start()

    def gather_plane(i):
        finish(i, 3)
        for j in range(3):
            p1_copy(i, j).wait_recv()
        kept[i * 4 + 3] += part1[i * 3] + part1[i * 3 + 1] + part1[i * 3 + 2]

    def leaf_copy(k):
        if k == 0:
            return [remote(sums.at[0], leaf_mate, leaf_ss.at[0], leaf_rs.at[0], sibling)]
        axis, dst = (inner, leaf_in) if k == 1 else (outer, leaf_out)
        return [remote(sums.at[k], dst.at[d - 1], leaf_ss.at[3 * k - 3 + d], leaf_rs.at[3 * k - 3 + d], axis(d)) for d in (1, 2, 3)]

    def leaves_0():
        for copy in route2:
            copy.wait_recv()
        right2 = jnp.where(x2[0] + x2[1] + x2[2] + x2[3] > 0.5, 1.0, 0.0)
        dir_s[0] = right2
        slot = iota((8, count), 0)
        sides = jnp.where(slot == 0, right2, jnp.where(slot == 1, 1.0 - right2, 0.0)).astype(bf16)
        sums[...] = jnp.zeros_like(sums)
        sums[0, :, 0:8] = lax.dot_general(w_s[...], sides, NT, preferred_element_type=f32)
        leaf_copy(0)[0].start()

    def leaves_1():
        leaf_copy(0)[0].wait_recv()
        sums[1] = sums[0] + leaf_mate[...]
        for copy in leaf_copy(1):
            copy.start()

    def leaves_2():
        for copy in leaf_copy(1):
            copy.wait_recv()
        sums[2] = sums[1] + leaf_in[0] + leaf_in[1] + leaf_in[2]
        for copy in leaf_copy(2):
            copy.start()

    def leaves_3():
        for copy in leaf_copy(2):
            copy.wait_recv()
        total = sums[2] + leaf_out[0] + leaf_out[1] + leaf_out[2]
        weight = -RATE * total[0:16] / (total[16:32] + LAMBDA)
        went = dir_s[0] > 0.5
        mine = dir_s[1] == iota((NODES2, count), 0).astype(f32)
        pick = jnp.where(went, weight[:, 0:1], weight[:, 1:2])
        out_margin[...] = rows[3:4, :] + jnp.sum(jnp.where(mine, pick, 0.0), axis=0, keepdims=True)

    def step(turn, carry):
        i, half = turn // 2, turn % 2
        for s in range(2):
            j = half * 2 + s
            t = i * 4 + j
            for dst, q in ((sent, 1 - c), (kept, c)):
                f = feature(i, j, q)
                for e in range(2):
                    dst[t, e, :, 0:LO * COLS] = histogram(f + e)
        for s in range(2):
            core_copy(i * 4 + half * 2 + s).start()

        @pl.when((turn > 0) & (half == 1))
        def _():
            pass_on(i, 0)
            pass_on(i, 1)

        @pl.when((turn > 0) & (half == 0))
        def _():
            pass_on(i - 1, 2)
            gather_plane(i - 1)
            p2_copy(i - 1).start()

        for k, action in enumerate((leaves_0, leaves_1, leaves_2, leaves_3)):
            pl.when(turn == k + 1)(action)
        return carry

    lax.fori_loop(0, 8, step, 0)
    pass_on(3, 2)
    gather_plane(3)
    for i in range(3):
        p2_copy(i).wait_recv()

    for e in range(2):
        hist = kept[15, e] + part2[0, e] + part2[1, e] + part2[2, e]
        a = hist.astype(bf16)
        rest = hist - a.astype(f32)
        b = rest.astype(bf16)
        d = (rest - b.astype(f32)).astype(bf16)
        total = jnp.zeros((COLS, B), f32)
        for k in range(LO):
            for piece in (d, b, a):
                total += lax.dot_general(piece, tri[k], TN, preferred_element_type=f32)[k * COLS:(k + 1) * COLS]
        g2, h2 = total[0:16], total[16:32]
        for grad_left, hess_left, out, stride in (
            (g2[0:8] + g2[8:16], h2[0:8] + h2[8:16], out1, 1), (g2, h2, out2, 2)):
            grad_total = grad_left[:, B - 1:B]
            hess_total = hess_left[:, B - 1:B]
            grad_right = grad_total - grad_left
            hess_right = hess_total - hess_left
            gain = (grad_left * grad_left / (hess_left + LAMBDA)
                    + grad_right * grad_right / (hess_right + LAMBDA)
                    - grad_total * grad_total / (hess_total + LAMBDA))
            for side in range(stride):
                for n in range(NODES1):
                    out[n * stride + side, e:e + 1, :] = gain[side * 8 + n:side * 8 + n + 1]

    for copy in route1 + route2 + leaf_copy(0) + leaf_copy(1) + leaf_copy(2):
        copy.wait_send()
    for t in range(16):
        core_copy(t).wait_send()
    for i in range(4):
        for j in range(3):
            p1_copy(i, j).wait_send()
    for i in range(3):
        p2_copy(i).wait_send()


def body(bins, grad, hess, margin, node_start, split_feat1, split_bin1, split_feat2, split_bin2):
    features, count = bins.shape
    rows = jnp.stack([grad.astype(f32), hess.astype(f32), node_start.astype(f32), margin])

    def by_side(a):
        return a.reshape(NODES1, 2).T.reshape(NODES2)

    pad = jnp.zeros((8,), jnp.int32)
    table = jnp.stack([
        jnp.concatenate([split_feat1, by_side(split_feat2), pad - 1]),
        jnp.concatenate([split_bin1, by_side(split_bin2), pad])], axis=1)
    own = features * 4 // 128
    dma = pltpu.SemaphoreType.DMA
    pair = (2, HI, 128)
    gain1, gain2, new_margin = pl.pallas_call(
        kernel,
        out_shape=(
            jax.ShapeDtypeStruct((NODES1, own, B), f32),
            jax.ShapeDtypeStruct((NODES2, own, B), f32),
            jax.ShapeDtypeStruct((1, count), f32)),
        in_specs=[pl.BlockSpec(memory_space=pltpu.VMEM)] * 3,
        out_specs=[pl.BlockSpec(memory_space=pltpu.VMEM)] * 3,
        scratch_shapes=[
            pltpu.VMEM((features, count), f32),
            pltpu.VMEM((features, count), f32),
            pltpu.VMEM((COLS, count), bf16),
            pltpu.VMEM((NODES2, count), f32),
            pltpu.VMEM((2, 1, count), f32),
            pltpu.VMEM((16,) + pair, f32),
            pltpu.VMEM((16,) + pair, f32),
            pltpu.VMEM((16,) + pair, f32),
            pltpu.VMEM((12,) + pair, f32),
            pltpu.VMEM((3,) + pair, f32),
            pltpu.VMEM((3, COLS, 128), f32),
            pltpu.VMEM((LO, HI, B), bf16),
            pltpu.VMEM((4, 1, count), f32),
            pltpu.VMEM((4, 1, count), f32),
            pltpu.VMEM((COLS, 128), f32),
            pltpu.VMEM((3, COLS, 128), f32),
            pltpu.VMEM((3, COLS, 128), f32),
            dma((3,)), dma((3,)), dma((3,)), dma((3,)),
            dma((16,)), dma((16,)), dma((12,)), dma((12,)), dma((3,)), dma((3,)),
            dma((7,)), dma((7,)),
        ],
        compiler_params=pltpu.CompilerParams(
            collective_id=0, has_side_effects=True, vmem_limit_bytes=40 * 2**20),
        cost_estimate=pl.CostEstimate(flops=2 * 64 * 4096 * 8192, bytes_accessed=2**20, transcendentals=0),
    )(bins, rows, table)
    return gain1, gain2, new_margin.reshape(count)


def solution(mesh):
    return jax.shard_map(
        body,
        mesh=mesh,
        in_specs=(P("feat", "row"), P("row"), P("row"), P("row"), P("row"), P(), P(), P(), P()),
        out_specs=(P(None, ("feat", "row"), None), P(None, ("feat", "row"), None), P("row")),
        check_vma=False,
    )
```

time: 309 us -> 55.9 us (0.18)
  the two profiles are of different devices: /device:TPU:1 before, /device:TPU:0 now
where the time goes in v1:
time: 55.9 us; the launch traced here: 55.4 us
  Pallas kernels  47 us (84%)
  local copies, waits for them, and re-layouts  7.56 us (14%)
  between operations  0.68 us (1%)
    pallas_call x1, Pallas kernels, body(): pl.pallas_call(kernel, out_shape=(jax.ShapeDtypeStruct((NODES1, own, B),...  47 us
    unnamed x21, local copies, waits for them, and re-layouts  6.98 us

profile of v1, /device:TPU:0, one launch (start us, length us, event | category | flops | bytes accessed | tf_op | source)
XLA Modules:
  0.0 55.4 jit_solution(1354651153700036674)
XLA Ops:
  0.6 0.6 %copy-done.5 = s32[16]{0:T(128)S(1)} copy-done((s32[16]{0:T(128)S(1)}, s32[16]{0:T(128)}, u32[]{:S(2)}) %copy-start.5) | copy-done | bytes 88
  1.3 0.1 reshape.21
  1.4 0.1 copy.20
  1.5 0.1 reshape.22
  1.5 0.6 %copy-done.6 = s32[16]{0:T(128)S(1)} copy-done((s32[16]{0:T(128)S(1)}, s32[16]{0:T(128)}, u32[]{:S(2)}) %copy-start.6) | copy-done | bytes 88
  2.1 0.1 reshape.23
  2.2 0.1 copy.21
  2.3 0.1 reshape.24
  2.4 0.7 %copy-done.7 = s32[8]{0:T(128)S(1)} copy-done((s32[8]{0:T(128)S(1)}, s32[8]{0:T(128)}, u32[]{:S(2)}) %copy-start.7) | copy-done | bytes 56
  3.0 0.0 copy-done.8
  3.0 0.1 add_bitcast_fusion
  3.1 0.0 copy-start.3
  3.1 0.1 copy.22.table
  3.2 0.6 %copy-done.3 = bf16[4096]{0:T(1024)(128)(2,1)S(1)} copy-done((bf16[4096]{0:T(1024)(128)(2,1)S(1)}, bf16[4096]{0:T(1024)(128)(2,1)}, u32[]{:S(2)}) %copy-start.3) | copy-done | bytes 8216
  3.8 0.7 %copy-done.4 = bf16[4096]{0:T(1024)(128)(2,1)S(1)} copy-done((bf16[4096]{0:T(1024)(128)(2,1)S(1)}, bf16[4096]{0:T(1024)(128)(2,1)}, u32[]{:S(2)}) %copy-start.4) | copy-done | bytes 8216
  4.5 0.0 copy-done.1
  4.6 0.7 %copy-done.2 = f32[4096]{0:T(1024)S(1)} copy-done((f32[4096]{0:T(1024)S(1)}, f32[4096]{0:T(1024)}, u32[]{:S(2)}) %copy-start.2) | copy-done | bytes 16408
  5.3 0.1 pad_maximum_fusion.rows
  5.3 0.0 copy-start
  5.4 1.2 %copy-done = s32[64,4096]{1,0:T(8,128)S(1)} copy-done((s32[64,4096]{1,0:T(8,128)S(1)}, s32[64,4096]{1,0:T(8,128)}, u32[]{:S(2)}) %copy-start) | copy-done | bytes 1048600
  6.6 47.0 %shard_map.112 = (f32[8,2,256]{2,1,0:T(2,128)S(1)}, f32[16,2,256]{2,1,0:T(2,128)S(1)}, f32[1,4096]{1,0:T(1,128)S(1)}) custom-call(s32[64,4096]{1,0:T(8,128)S(1)} %copy-done, f32[4,4096]{1,0:T(4,128)S(1)} %pad_maximum_fusion.rows, s32[32,2]{1,0:T(8,128)S(1)} %copy.22.table), custom_call_target="tpu_custom_call" | custom-call | flops 4294967296 | bytes 1048576 | tf_op jit(solution)/shard_map/pallas_call | solution.py:253
  53.6 0.6 %copy.26 = f32[8,2,256]{2,1,0:T(2,128)} copy(f32[8,2,256]{2,1,0:T(2,128)S(1)} %get-tuple-element.14) | data formatting | bytes 32768
  54.2 0.6 %copy.27 = f32[16,2,256]{2,1,0:T(2,128)} copy(f32[16,2,256]{2,1,0:T(2,128)S(1)} %get-tuple-element.15) | data formatting | bytes 65536
  54.8 0.6 %copy.28 = f32[4096]{0:T(1024)} copy(f32[4096]{0:T(1024)S(1)} %bitcast.11) | data formatting | bytes 32768
  (13 shorter events, 0.0 us)
Async XLA Ops:
  0.6 0.7 %copy-start.5 = (s32[16]{0:T(128)S(1)}, s32[16]{0:T(128)}, u32[]{:S(2)}) copy-start(s32[16]{0:T(128)} %param.16) | copy-start | bytes 196
  1.4 0.7 %copy-start.6 = (s32[16]{0:T(128)S(1)}, s32[16]{0:T(128)}, u32[]{:S(2)}) copy-start(s32[16]{0:T(128)} %param.17) | copy-start | bytes 196
  2.4 0.7 %copy-start.7 = (s32[8]{0:T(128)S(1)}, s32[8]{0:T(128)}, u32[]{:S(2)}) copy-start(s32[8]{0:T(128)} %param.14) | copy-start | bytes 100
  2.4 0.7 %copy-start.8 = (s32[8]{0:T(128)S(1)}, s32[8]{0:T(128)}, u32[]{:S(2)}) copy-start(s32[8]{0:T(128)} %param.15) | copy-start | bytes 100
  3.1 0.7 %copy-start.3 = (bf16[4096]{0:T(1024)(128)(2,1)S(1)}, bf16[4096]{0:T(1024)(128)(2,1)}, u32[]{:S(2)}) copy-start(bf16[4096]{0:T(1024)(128)(2,1)} %param.10) | copy-start | bytes 24580
  3.8 0.7 %copy-start.4 = (bf16[4096]{0:T(1024)(128)(2,1)S(1)}, bf16[4096]{0:T(1024)(128)(2,1)}, u32[]{:S(2)}) copy-start(bf16[4096]{0:T(1024)(128)(2,1)} %param.11) | copy-start | bytes 24580
  3.8 0.7 %copy-start.1 = (s32[4096]{0:T(1024)S(1)}, s32[4096]{0:T(1024)}, u32[]{:S(2)}) copy-start(s32[4096]{0:T(1024)} %param.13) | copy-start | bytes 49156
  4.6 0.7 %copy-start.2 = (f32[4096]{0:T(1024)S(1)}, f32[4096]{0:T(1024)}, u32[]{:S(2)}) copy-start(f32[4096]{0:T(1024)} %param.12) | copy-start | bytes 49156
  5.3 1.2 %copy-start = (s32[64,4096]{1,0:T(8,128)S(1)}, s32[64,4096]{1,0:T(8,128)}, u32[]{:S(2)}) copy-start(s32[64,4096]{1,0:T(8,128)} %bins.1) | copy-start | bytes 3145732

commit v2 on v1

--- a/solution.py
+++ b/solution.py
@@ -28,11 +28,20 @@
     return lax.broadcasted_iota(jnp.int32, shape, dim)
 
 
-def kernel(bins, rows, table, out1, out2, out_margin,
-           hi_s, lo_s, w_s, picked_s, dir_s, kept, sent, mate, part1, part2, sums, tri,
+def kernel(bins_hbm, grad_hbm, hess_hbm, margin_hbm, node_hbm, feat1, bin1, feat2, bin2, out1, out2, out_margin,
+           bins, grad, hess, margin, node_in, packed, in_sem, hi_s, lo_s, w_s, picked_s, dir_s, kept, sent, mate, part1, part2, sums, tri,
            x1, x2, leaf_mate, leaf_in, leaf_out,
            x1_ss, x1_rs, x2_ss, x2_rs, core_ss, core_rs, p1_ss, p1_rs, p2_ss, p2_rs, leaf_ss, leaf_rs):
     features, count = bins.shape
+    lines = count // 128
+    loads = [pltpu.make_async_copy(src, dst, in_sem.at[k]) for k, (src, dst) in enumerate((
+        (bins_hbm, bins), (node_hbm, node_in), (grad_hbm, grad), (hess_hbm, hess), (margin_hbm, margin)))]
+    for copy in loads:
+        copy.start()
+
+    def row(k):
+        return jnp.concatenate([packed[k, r:r + 1, :] for r in range(lines)], axis=1)
+
     me = lax.axis_index("row")
     feat = lax.axis_index("feat")
     z, y, c = me // 8, (me // 2) % 4, me % 2
@@ -43,12 +52,16 @@
     def outer(d):
         return (((z + d * (1 - c)) % 4) * 8 + ((y + d * c) % 4) * 2 + c, feat)
 
+    def cross(d, q):
+        return (((z + d * q) % 4) * 8 + ((y + d * (1 - q)) % 4) * 2 + q, feat)
+
     sibling = (z * 8 + y * 2 + (1 - c), feat)
 
     def across(d):
         return (me, (feat + d) % 4)
 
     peers = [sibling] + [axis(d) for axis in (inner, outer, across) for d in (1, 2, 3)]
+    peers.append((((z + c) % 4) * 8 + ((y + 1 - c) % 4) * 2 + 1 - c, feat))
     barrier = pltpu.get_barrier_semaphore()
     for peer in peers:
         pl.semaphore_signal(barrier, inc=1, device_id=peer, device_id_type=MESH)
@@ -57,12 +70,28 @@
         return pltpu.make_async_remote_copy(
             src_ref=src, dst_ref=dst, send_sem=ss, recv_sem=rs, device_id=peer, device_id_type=MESH)
 
-    local = table[:, 0:1] - feat * features
-    select = jnp.where(local == iota((32, features), 1), 1.0, 0.0).astype(bf16)
+    line = iota((32, 128), 0)
+    owner = jnp.full((32, 128), -1, jnp.int32)
+    cut = jnp.zeros((32, 128), jnp.int32)
+    for n in range(NODES1):
+        owner = jnp.where(line == n, feat1[n], owner)
+        cut = jnp.where(line == n, bin1[n], cut)
+    for n in range(NODES2):
+        at = 8 + (n % 2) * 8 + n // 2
+        owner = jnp.where(line == at, feat2[n], owner)
+        cut = jnp.where(line == at, bin2[n], cut)
+    local = owner - feat * features
+    select = jnp.where(local == iota((32, 128), 1), 1.0, 0.0).astype(bf16)[:, 0:features]
+    for copy in loads:
+        copy.wait()
+    packed[0] = grad[...].astype(f32)
+    packed[1] = hess[...].astype(f32)
+    packed[2] = node_in[...].astype(f32)
+    packed[3] = margin[...]
     values = bins[...].astype(f32)
     picked = lax.dot_general(select, values.astype(bf16), (((1,), (0,)), ((), ())), preferred_element_type=f32)
-    above = jnp.where(picked > table[:, 1:2].astype(f32), 1.0, 0.0)
-    node = rows[2:3, :]
+    above = jnp.where(picked > cut[:, 0:1].astype(f32), 1.0, 0.0)
+    node = row(2)
     first = node == iota((NODES1, count), 0).astype(f32)
     x1[3] = jnp.max(jnp.where(first, above[0:8], 0.0), axis=0, keepdims=True)
     picked_s[...] = above[8:24]
@@ -83,8 +112,8 @@
     child = jnp.where(right > 0.5, 8.0, 0.0) + node
     member = child == iota((NODES2, count), 0).astype(f32)
     dir_s[1] = child
-    w_s[0:16, :] = jnp.where(member, rows[0:1, :], 0.0).astype(bf16)
-    w_s[16:32, :] = jnp.where(member, rows[1:2, :], 0.0).astype(bf16)
+    w_s[0:16, :] = jnp.where(member, row(0), 0.0).astype(bf16)
+    w_s[16:32, :] = jnp.where(member, row(1), 0.0).astype(bf16)
     x2[3] = jnp.max(jnp.where(member, picked_s[...], 0.0), axis=0, keepdims=True)
     route2 = [remote(x2.at[3], x2.at[d - 1], x2_ss.at[d - 1], x2_rs.at[d - 1], across(d)) for d in (1, 2, 3)]
     for copy in route2:
@@ -107,26 +136,24 @@
     def core_copy(t):
         return remote(sent.at[t], mate.at[t], core_ss.at[t], core_rs.at[t], sibling)
 
-    def p1_copy(i, j):
-        return remote(kept.at[i * 4 + j], part1.at[i * 3 + j], p1_ss.at[i * 3 + j], p1_rs.at[i * 3 + j], inner(j + 1))
+    def p1_copy(t, slot, j):
+        return remote(kept.at[t], part1.at[slot], p1_ss.at[slot], p1_rs.at[slot], inner(j + 1))
+
+    def cross_copy():
+        return remote(sent.at[14], part1.at[12], p1_ss.at[12], p1_rs.at[12], cross(3, 1 - c))
 
     def p2_copy(i):
-        return remote(kept.at[i * 4 + 3], part2.at[i], p2_ss.at[i], p2_rs.at[i], outer(i + 1))
-
-    def finish(i, j):
-        t = i * 4 + j
+        return remote(kept.at[9 + i], part2.at[i], p2_ss.at[i], p2_rs.at[i], outer(i + 1))
+
+    def finish(t):
         core_copy(t).wait_recv()
         kept[t] += mate[t]
 
-    def pass_on(i, j):
-        finish(i, j)
-        p1_copy(i, j).start()
-
     def gather_plane(i):
-        finish(i, 3)
         for j in range(3):
-            p1_copy(i, j).wait_recv()
-        kept[i * 4 + 3] += part1[i * 3] + part1[i * 3 + 1] + part1[i * 3 + 2]
+            p1_copy(0, i * 3 + j, j).wait_recv()
+        kept[9 + i] += part1[i * 3] + part1[i * 3 + 1] + part1[i * 3 + 2]
+        p2_copy(i).start()
 
     def leaf_copy(k):
         if k == 0:
@@ -166,43 +193,75 @@
         went = dir_s[0] > 0.5
         mine = dir_s[1] == iota((NODES2, count), 0).astype(f32)
         pick = jnp.where(went, weight[:, 0:1], weight[:, 1:2])
-        out_margin[...] = rows[3:4, :] + jnp.sum(jnp.where(mine, pick, 0.0), axis=0, keepdims=True)
+        result = row(3) + jnp.sum(jnp.where(mine, pick, 0.0), axis=0, keepdims=True)
+        for r in range(lines):
+            out_margin[r:r + 1, :] = result[:, r * 128:(r + 1) * 128]
+
+    def place(t):
+        own = t // 9
+        k, r = (t - 9 * own) // 3, (t - 9 * own) % 3
+        k0, k1 = (2 - k) // 2, k % 2
+        return (1 - own) * k + own * (k0 * r + (1 - k0) * 3), (1 - own) * r + own * (k1 * r + (1 - k1) * 3)
 
     def step(turn, carry):
-        i, half = turn // 2, turn % 2
         for s in range(2):
-            j = half * 2 + s
-            t = i * 4 + j
+            t = turn * 2 + s
+            i, j = place(t)
             for dst, q in ((sent, 1 - c), (kept, c)):
                 f = feature(i, j, q)
                 for e in range(2):
                     dst[t, e, :, 0:LO * COLS] = histogram(f + e)
-        for s in range(2):
-            core_copy(i * 4 + half * 2 + s).start()
-
-        @pl.when((turn > 0) & (half == 1))
-        def _():
-            pass_on(i, 0)
-            pass_on(i, 1)
-
-        @pl.when((turn > 0) & (half == 0))
-        def _():
-            pass_on(i - 1, 2)
-            gather_plane(i - 1)
-            p2_copy(i - 1).start()
+
+        @pl.when(turn < 7)
+        def _():
+            for s in range(2):
+                core_copy(turn * 2 + s).start()
+
+        @pl.when((turn > 0) & (turn < 5))
+        def _():
+            for s in range(2):
+                t = turn * 2 - 2 + s
+                finish(t)
+                p1_copy(t, t, t % 3).start()
+
+        @pl.when(turn == 5)
+        def _():
+            finish(8)
+            p1_copy(8, 8, 2).start()
+            finish(9)
+            gather_plane(0)
+
+        @pl.when(turn == 6)
+        def _():
+            finish(10)
+            gather_plane(1)
+            finish(11)
+
+        @pl.when(turn == 7)
+        def _():
+            core_copy(15).start()
+            p1_copy(14, 11, 2).start()
+            cross_copy().start()
+            for j in range(2):
+                finish(12 + j)
+                p1_copy(12 + j, 9 + j, j).start()
+            gather_plane(2)
 
         for k, action in enumerate((leaves_0, leaves_1, leaves_2, leaves_3)):
-            pl.when(turn == k + 1)(action)
+            pl.when(turn == (1, 2, 4, 6)[k])(action)
         return carry
 
     lax.fori_loop(0, 8, step, 0)
-    pass_on(3, 2)
-    gather_plane(3)
+    finish(15)
     for i in range(3):
         p2_copy(i).wait_recv()
+    for j in range(3):
+        p1_copy(12 + j, 9 + j, j).wait_recv()
+    cross_copy().wait_recv()
 
     for e in range(2):
-        hist = kept[15, e] + part2[0, e] + part2[1, e] + part2[2, e]
+        hist = (kept[15, e] + part2[0, e] + part2[1, e] + part2[2, e]
+                + part1[9, e] + part1[10, e] + part1[11, e] + part1[12, e])
         a = hist.astype(bf16)
         rest = hist - a.astype(f32)
         b = rest.astype(bf16)
@@ -227,26 +286,33 @@
 
     for copy in route1 + route2 + leaf_copy(0) + leaf_copy(1) + leaf_copy(2):
         copy.wait_send()
-    for t in range(16):
+    for t in list(range(14)) + [15]:
         core_copy(t).wait_send()
-    for i in range(4):
-        for j in range(3):
-            p1_copy(i, j).wait_send()
+    for t in list(range(9)) + [12, 13, 14]:
+        p1_copy(t, t if t < 9 else t - 3, t % 3).wait_send()
+    cross_copy().wait_send()
     for i in range(3):
         p2_copy(i).wait_send()
 
 
+def copy_kernel(a, b, d, a_out, b_out, d_out):
+    for src, dst in ((a, a_out), (b, b_out), (d, d_out)):
+        dst[...] = src[...]
+
+
+def hand_out(*arrays):
+    return pl.pallas_call(
+        copy_kernel,
+        out_shape=tuple(jax.ShapeDtypeStruct(a.shape, a.dtype) for a in arrays),
+        in_specs=[pl.BlockSpec(memory_space=pltpu.VMEM)] * 3,
+        out_specs=[pl.BlockSpec(memory_space=pltpu.VMEM)] * 3,
+        name="hand_out",
+    )(*arrays)
+
+
 def body(bins, grad, hess, margin, node_start, split_feat1, split_bin1, split_feat2, split_bin2):
     features, count = bins.shape
-    rows = jnp.stack([grad.astype(f32), hess.astype(f32), node_start.astype(f32), margin])
-
-    def by_side(a):
-        return a.reshape(NODES1, 2).T.reshape(NODES2)
-
-    pad = jnp.zeros((8,), jnp.int32)
-    table = jnp.stack([
-        jnp.concatenate([split_feat1, by_side(split_feat2), pad - 1]),
-        jnp.concatenate([split_bin1, by_side(split_bin2), pad])], axis=1)
+    lines = (count // 128, 128)
     own = features * 4 // 128
     dma = pltpu.SemaphoreType.DMA
     pair = (2, HI, 128)
@@ -255,10 +321,17 @@
         out_shape=(
             jax.ShapeDtypeStruct((NODES1, own, B), f32),
             jax.ShapeDtypeStruct((NODES2, own, B), f32),
-            jax.ShapeDtypeStruct((1, count), f32)),
-        in_specs=[pl.BlockSpec(memory_space=pltpu.VMEM)] * 3,
+            jax.ShapeDtypeStruct(lines, f32)),
+        in_specs=[pl.BlockSpec(memory_space=pltpu.HBM)] * 5 + [pl.BlockSpec(memory_space=pltpu.SMEM)] * 4,
         out_specs=[pl.BlockSpec(memory_space=pltpu.VMEM)] * 3,
         scratch_shapes=[
+            pltpu.VMEM((features, count), jnp.int32),
+            pltpu.VMEM(lines, bf16),
+            pltpu.VMEM(lines, bf16),
+            pltpu.VMEM(lines, f32),
+            pltpu.VMEM(lines, jnp.int32),
+            pltpu.VMEM((4,) + lines, f32),
+            dma((5,)),
             pltpu.VMEM((features, count), f32),
             pltpu.VMEM((features, count), f32),
             pltpu.VMEM((COLS, count), bf16),
@@ -267,7 +340,7 @@
             pltpu.VMEM((16,) + pair, f32),
             pltpu.VMEM((16,) + pair, f32),
             pltpu.VMEM((16,) + pair, f32),
-            pltpu.VMEM((12,) + pair, f32),
+            pltpu.VMEM((13,) + pair, f32),
             pltpu.VMEM((3,) + pair, f32),
             pltpu.VMEM((3, COLS, 128), f32),
             pltpu.VMEM((LO, HI, B), bf16),
@@ -277,13 +350,15 @@
             pltpu.VMEM((3, COLS, 128), f32),
             pltpu.VMEM((3, COLS, 128), f32),
             dma((3,)), dma((3,)), dma((3,)), dma((3,)),
-            dma((16,)), dma((16,)), dma((12,)), dma((12,)), dma((3,)), dma((3,)),
+            dma((16,)), dma((16,)), dma((13,)), dma((13,)), dma((3,)), dma((3,)),
             dma((7,)), dma((7,)),
         ],
         compiler_params=pltpu.CompilerParams(
-            collective_id=0, has_side_effects=True, vmem_limit_bytes=40 * 2**20),
+            collective_id=0, has_side_effects=True, vmem_limit_bytes=60 * 2**20),
         cost_estimate=pl.CostEstimate(flops=2 * 64 * 4096 * 8192, bytes_accessed=2**20, transcendentals=0),
-    )(bins, rows, table)
+    )(bins, grad.reshape(lines), hess.reshape(lines), margin.reshape(lines), node_start.reshape(lines),
+      split_feat1, split_bin1, split_feat2, split_bin2)
+    gain1, gain2, new_margin = hand_out(gain1, gain2, new_margin)
     return gain1, gain2, new_margin.reshape(count)
 
 

time: 55.9 us -> 37.6 us (0.67)
  the two profiles are of different devices: /device:TPU:0 before, /device:TPU:1 now
where the time goes in v2:
time: 37.6 us; the launch traced here: 37.3 us
  Pallas kernels  36.7 us (98%)
  between operations  0.64 us (2%)
    pallas_call x1, Pallas kernels, body(): pl.pallas_call(kernel, out_shape=(jax.ShapeDtypeStruct((NODES1, own, B),...  35.3 us
    pallas_call x1, Pallas kernels, hand_out(): pl.pallas_call(copy_kernel, out_shape=tuple((jax.ShapeDtypeStruct(a.shape...  1.39 us

profile of v2, /device:TPU:1, one launch (start us, length us, event | category | flops | bytes accessed | tf_op | source)
XLA Modules:
  0.0 37.3 jit_solution(15774052311576864129)
XLA Ops:
  0.6 35.3 %shard_map.112 = (f32[8,2,256]{2,1,0:T(2,128)}, f32[16,2,256]{2,1,0:T(2,128)}, f32[32,128]{1,0:T(8,128)}) custom-call(s32[64,4096]{1,0:T(8,128)} %bins_hbm.1, bf16[32,128]{1,0:T(8,128)(2,1)} %bitcast.8, bf16[32,128]{1,0:T(8,128)(2,1)} %bitcast.9, f32[32,128]{1,0:T(8,128)} %bitcast.5, s32[32,128]{1,0:T(8,128)} %bitcast.6, s32[8]{0:T(128)} %feat1.1, s32[8]{0:T(128)} %bin1.1, ...), custom_call_target="tpu_custom_call" | custom-call | flops 4294967296 | bytes 1048576 | tf_op jit(solution)/shard_map/pallas_call | solution.py:319
  36.0 1.4 %hand_out.1 = (f32[8,2,256]{2,1,0:T(2,128)}, f32[16,2,256]{2,1,0:T(2,128)}, f32[32,128]{1,0:T(8,128)}) custom-call(f32[8,2,256]{2,1,0:T(2,128)} %get-tuple-element.9.a, f32[16,2,256]{2,1,0:T(2,128)} %get-tuple-element.10.b, f32[32,128]{1,0:T(8,128)} %get-tuple-element.11.d), custom_call_target="tpu_custom_call" | custom-call | tf_op jit(solution)/shard_map/hand_out/pallas_call | solution.py:304

commit v3 on v2

--- a/solution.py
+++ b/solution.py
@@ -13,9 +13,10 @@
 
 SEG = 86
 HI = 88
+FOLD = 48
 LO = 3
 COLS = 2 * NODES2
-UNROLL = 8
+OWN = (9, 10, 12)
 
 MESH = pl.DeviceIdType.MESH
 NT = (((1,), (1,)), ((), ()))
@@ -30,7 +31,7 @@
 
 def kernel(bins_hbm, grad_hbm, hess_hbm, margin_hbm, node_hbm, feat1, bin1, feat2, bin2, out1, out2, out_margin,
            bins, grad, hess, margin, node_in, packed, in_sem, hi_s, lo_s, w_s, picked_s, dir_s, kept, sent, mate, part1, part2, sums, tri,
-           x1, x2, leaf_mate, leaf_in, leaf_out,
+           x1, x2, leaf_mate, leaf_in, leaf_out, wide,
            x1_ss, x1_rs, x2_ss, x2_rs, core_ss, core_rs, p1_ss, p1_rs, p2_ss, p2_rs, leaf_ss, leaf_rs):
     features, count = bins.shape
     lines = count // 128
@@ -61,7 +62,7 @@
         return (me, (feat + d) % 4)
 
     peers = [sibling] + [axis(d) for axis in (inner, outer, across) for d in (1, 2, 3)]
-    peers.append((((z + c) % 4) * 8 + ((y + 1 - c) % 4) * 2 + 1 - c, feat))
+    peers.append((((z + 3 * c) % 4) * 8 + ((y + 3 - 3 * c) % 4) * 2 + 1 - c, feat))
     barrier = pltpu.get_barrier_semaphore()
     for peer in peers:
         pl.semaphore_signal(barrier, inc=1, device_id=peer, device_id_type=MESH)
@@ -103,9 +104,9 @@
     lo = jnp.where(values >= 2.0 * SEG, 2.0, jnp.where(values >= 1.0 * SEG, 1.0, 0.0))
     lo_s[...] = lo
     hi_s[...] = values - SEG * lo
-    h = iota((HI, B), 0)
+    h = iota((2 * FOLD, B), 0)
     for k in range(LO):
-        tri[k] = jnp.where((h + k * SEG <= iota((HI, B), 1)) & (h < SEG), 1.0, 0.0).astype(bf16)
+        tri[k] = jnp.where((h + k * SEG <= iota((2 * FOLD, B), 1)) & (h < SEG), 1.0, 0.0).astype(bf16)
     for copy in route1:
         copy.wait_recv()
     right = x1[0] + x1[1] + x1[2] + x1[3]
@@ -140,10 +141,10 @@
         return remote(kept.at[t], part1.at[slot], p1_ss.at[slot], p1_rs.at[slot], inner(j + 1))
 
     def cross_copy():
-        return remote(sent.at[14], part1.at[12], p1_ss.at[12], p1_rs.at[12], cross(3, 1 - c))
+        return remote(sent.at[14], part1.at[12], p1_ss.at[12], p1_rs.at[12], cross(1, 1 - c))
 
     def p2_copy(i):
-        return remote(kept.at[9 + i], part2.at[i], p2_ss.at[i], p2_rs.at[i], outer(i + 1))
+        return remote(kept.at[OWN[i]], part2.at[i], p2_ss.at[i], p2_rs.at[i], outer(i + 1))
 
     def finish(t):
         core_copy(t).wait_recv()
@@ -152,7 +153,7 @@
     def gather_plane(i):
         for j in range(3):
             p1_copy(0, i * 3 + j, j).wait_recv()
-        kept[9 + i] += part1[i * 3] + part1[i * 3 + 1] + part1[i * 3 + 2]
+        kept[OWN[i]] += part1[i * 3] + part1[i * 3 + 1] + part1[i * 3 + 2]
         p2_copy(i).start()
 
     def leaf_copy(k):
@@ -198,24 +199,36 @@
             out_margin[r:r + 1, :] = result[:, r * 128:(r + 1) * 128]
 
     def place(t):
-        own = t // 9
-        k, r = (t - 9 * own) // 3, (t - 9 * own) % 3
-        k0, k1 = (2 - k) // 2, k % 2
-        return (1 - own) * k + own * (k0 * r + (1 - k0) * 3), (1 - own) * r + own * (k1 * r + (1 - k1) * 3)
+        own, v = t // 9, t % 9
+        late = v // 4
+        mid = (v // 2) * (1 - late)
+        at2, at3 = mid * (1 - v % 2), mid * (v % 2)
+        i = (1 - own) * (v // 3) + own * (v + at2 - at3 - late)
+        j = (1 - own) * (v % 3) + own * (3 - 2 * at2 - late)
+        return i, j
+
+    def fill(dst, t, f):
+        for e in range(2):
+            wide[e, :, 0:LO * COLS] = histogram(f + e)
+        one, two = wide[0], wide[1]
+        lane = iota((HI, 128), 1)
+        dst[t, 0:HI] = jnp.where(lane < LO * COLS, one, pltpu.roll(two, COLS, 1))
+        below = jnp.concatenate([two[FOLD:HI], jnp.zeros((2 * FOLD - HI, 128), f32)], 0)
+        dst[t, HI:HI + FOLD] = jnp.where(lane[0:FOLD] < 64, two[0:FOLD], pltpu.roll(below, 64, 1))
+
+    def compute_sent(t, i, j):
+        fill(sent, t, feature(i, j, 1 - c))
+
+    def compute_kept(t, i, j):
+        fill(kept, t, feature(i, j, c))
 
     def step(turn, carry):
         for s in range(2):
             t = turn * 2 + s
-            i, j = place(t)
-            for dst, q in ((sent, 1 - c), (kept, c)):
-                f = feature(i, j, q)
-                for e in range(2):
-                    dst[t, e, :, 0:LO * COLS] = histogram(f + e)
-
-        @pl.when(turn < 7)
-        def _():
-            for s in range(2):
-                core_copy(turn * 2 + s).start()
+            compute_sent(t, *place(t))
+            compute_kept(t, *place(t))
+        for s in range(2):
+            core_copy(turn * 2 + s).start()
 
         @pl.when((turn > 0) & (turn < 5))
         def _():
@@ -233,43 +246,54 @@
 
         @pl.when(turn == 6)
         def _():
+            finish(11)
+            p1_copy(11, 9, 1).start()
             finish(10)
             gather_plane(1)
-            finish(11)
-
-        @pl.when(turn == 7)
-        def _():
-            core_copy(15).start()
-            p1_copy(14, 11, 2).start()
-            cross_copy().start()
-            for j in range(2):
-                finish(12 + j)
-                p1_copy(12 + j, 9 + j, j).start()
-            gather_plane(2)
-
-        for k, action in enumerate((leaves_0, leaves_1, leaves_2, leaves_3)):
-            pl.when(turn == (1, 2, 4, 6)[k])(action)
+
+        for k, action in enumerate((leaves_0, leaves_1, leaves_2)):
+            pl.when(turn == (1, 2, 4)[k])(action)
         return carry
 
-    lax.fori_loop(0, 8, step, 0)
+    lax.fori_loop(0, 7, step, 0)
+    compute_sent(14, 3, 0)
+    cross_copy().start()
+    compute_kept(14, 3, 0)
+    p1_copy(14, 11, 0).start()
+    finish(13)
+    p1_copy(13, 10, 2).start()
+    finish(12)
+    gather_plane(2)
+    compute_sent(15, 3, 3)
+    core_copy(15).start()
+    compute_kept(15, 3, 3)
+    leaves_3()
     finish(15)
     for i in range(3):
         p2_copy(i).wait_recv()
-    for j in range(3):
-        p1_copy(12 + j, 9 + j, j).wait_recv()
+    for t, slot, j in ((11, 9, 1), (13, 10, 2), (14, 11, 0)):
+        p1_copy(t, slot, j).wait_recv()
     cross_copy().wait_recv()
 
-    for e in range(2):
-        hist = (kept[15, e] + part2[0, e] + part2[1, e] + part2[2, e]
-                + part1[9, e] + part1[10, e] + part1[11, e] + part1[12, e])
-        a = hist.astype(bf16)
-        rest = hist - a.astype(f32)
+    hist = (kept[15] + part2[0] + part2[1] + part2[2] + part1[9] + part1[10] + part1[11] + part1[12])
+
+    def split(x):
+        a = x.astype(bf16)
+        rest = x - a.astype(f32)
         b = rest.astype(bf16)
-        d = (rest - b.astype(f32)).astype(bf16)
-        total = jnp.zeros((COLS, B), f32)
-        for k in range(LO):
-            for piece in (d, b, a):
-                total += lax.dot_general(piece, tri[k], TN, preferred_element_type=f32)[k * COLS:(k + 1) * COLS]
+        return (rest - b.astype(f32)).astype(bf16), b, a
+
+    def summed(pieces, ones):
+        return sum(lax.dot_general(piece, ones, TN, preferred_element_type=f32) for piece in pieces)
+
+    upper = split(jnp.concatenate([hist[0:HI], jnp.zeros((2 * FOLD - HI, 128), f32)], 0))
+    folded = split(hist[HI:HI + FOLD])
+    tops = [summed(upper, tri[k]) for k in range(LO)]
+    first_half = [summed(folded, tri[k, 0:FOLD]) for k in range(2)]
+    second_half = [summed(folded, tri[k, FOLD:2 * FOLD]) for k in range(2)]
+    totals = (tops[0][0:32] + tops[1][32:64] + tops[2][64:96],
+              first_half[0][0:32] + second_half[0][64:96] + first_half[1][32:64] + second_half[1][96:128] + tops[2][96:128])
+    for e, total in enumerate(totals):
         g2, h2 = total[0:16], total[16:32]
         for grad_left, hess_left, out, stride in (
             (g2[0:8] + g2[8:16], h2[0:8] + h2[8:16], out1, 1), (g2, h2, out2, 2)):
@@ -288,8 +312,10 @@
         copy.wait_send()
     for t in list(range(14)) + [15]:
         core_copy(t).wait_send()
-    for t in list(range(9)) + [12, 13, 14]:
-        p1_copy(t, t if t < 9 else t - 3, t % 3).wait_send()
+    for t in range(9):
+        p1_copy(t, t, t % 3).wait_send()
+    for t, slot, j in ((11, 9, 1), (13, 10, 2), (14, 11, 0)):
+        p1_copy(t, slot, j).wait_send()
     cross_copy().wait_send()
     for i in range(3):
         p2_copy(i).wait_send()
@@ -315,7 +341,7 @@
     lines = (count // 128, 128)
     own = features * 4 // 128
     dma = pltpu.SemaphoreType.DMA
-    pair = (2, HI, 128)
+    pair = (HI + FOLD, 128)
     gain1, gain2, new_margin = pl.pallas_call(
         kernel,
         out_shape=(
@@ -343,12 +369,13 @@
             pltpu.VMEM((13,) + pair, f32),
             pltpu.VMEM((3,) + pair, f32),
             pltpu.VMEM((3, COLS, 128), f32),
-            pltpu.VMEM((LO, HI, B), bf16),
+            pltpu.VMEM((LO, 2 * FOLD, B), bf16),
             pltpu.VMEM((4, 1, count), f32),
             pltpu.VMEM((4, 1, count), f32),
             pltpu.VMEM((COLS, 128), f32),
             pltpu.VMEM((3, COLS, 128), f32),
             pltpu.VMEM((3, COLS, 128), f32),
+            pltpu.VMEM((2, HI, 128), f32),
             dma((3,)), dma((3,)), dma((3,)), dma((3,)),
             dma((16,)), dma((16,)), dma((13,)), dma((13,)), dma((3,)), dma((3,)),
             dma((7,)), dma((7,)),

time: 37.6 us -> 36.6 us (0.973)
  Pallas kernels: 36.7 us -> 35.7 us
    pallas_call x1, Pallas kernels: 35.3 us -> 34.3 us  [body(): pl.pallas_call(kernel, out_shape=(jax.ShapeDtypeStruct((NODES1, own, B),...]
where the time goes in v3:
time: 36.6 us; the launch traced here: 36.4 us
  Pallas kernels  35.7 us (98%)
  between operations  0.64 us (2%)
    pallas_call x1, Pallas kernels, body(): pl.pallas_call(kernel, out_shape=(jax.ShapeDtypeStruct((NODES1, own, B),...  34.3 us
    pallas_call x1, Pallas kernels, hand_out(): pl.pallas_call(copy_kernel, out_shape=tuple((jax.ShapeDtypeStruct(a.shape...  1.39 us

profile of v3, /device:TPU:1, one launch (start us, length us, event | category | flops | bytes accessed | tf_op | source)
XLA Modules:
  0.0 36.4 jit_solution(3949963029621685155)
XLA Ops:
  0.6 34.3 %shard_map.112 = (f32[8,2,256]{2,1,0:T(2,128)}, f32[16,2,256]{2,1,0:T(2,128)}, f32[32,128]{1,0:T(8,128)}) custom-call(s32[64,4096]{1,0:T(8,128)} %bins_hbm.1, bf16[32,128]{1,0:T(8,128)(2,1)} %bitcast.8, bf16[32,128]{1,0:T(8,128)(2,1)} %bitcast.9, f32[32,128]{1,0:T(8,128)} %bitcast.5, s32[32,128]{1,0:T(8,128)} %bitcast.6, s32[8]{0:T(128)} %feat1.1, s32[8]{0:T(128)} %bin1.1, ...), custom_call_target="tpu_custom_call" | custom-call | flops 4294967296 | bytes 1048576 | tf_op jit(solution)/shard_map/pallas_call | solution.py:345
  35.0 1.4 %hand_out.1 = (f32[8,2,256]{2,1,0:T(2,128)}, f32[16,2,256]{2,1,0:T(2,128)}, f32[32,128]{1,0:T(8,128)}) custom-call(f32[8,2,256]{2,1,0:T(2,128)} %get-tuple-element.9.a, f32[16,2,256]{2,1,0:T(2,128)} %get-tuple-element.10.b, f32[32,128]{1,0:T(8,128)} %get-tuple-element.11.d), custom_call_target="tpu_custom_call" | custom-call | tf_op jit(solution)/shard_map/hand_out/pallas_call | solution.py:330

commit v4 on v3

--- a/solution.py
+++ b/solution.py
@@ -29,14 +29,19 @@
     return lax.broadcasted_iota(jnp.int32, shape, dim)
 
 
-def kernel(bins_hbm, grad_hbm, hess_hbm, margin_hbm, node_hbm, feat1, bin1, feat2, bin2, out1, out2, out_margin,
-           bins, grad, hess, margin, node_in, packed, in_sem, hi_s, lo_s, w_s, picked_s, dir_s, kept, sent, mate, part1, part2, sums, tri,
+def kernel(bins_hbm, grad_hbm, hess_hbm, margin_hbm, node_hbm, feat1_hbm, bin1_hbm, feat2_hbm, bin2_hbm,
+           out1_hbm, out2_hbm, margin_out_hbm,
+           bins, grad, hess, margin, node_in, feat1, bin1, feat2, bin2, out1, out2, out_margin,
+           packed, first_s, in_sem, out_sem, hi_s, lo_s, w_s, picked_s, dir_s, kept, sent, mate, part1, part2, sums, tri,
            x1, x2, leaf_mate, leaf_in, leaf_out, wide,
            x1_ss, x1_rs, x2_ss, x2_rs, core_ss, core_rs, p1_ss, p1_rs, p2_ss, p2_rs, leaf_ss, leaf_rs):
     features, count = bins.shape
     lines = count // 128
     loads = [pltpu.make_async_copy(src, dst, in_sem.at[k]) for k, (src, dst) in enumerate((
-        (bins_hbm, bins), (node_hbm, node_in), (grad_hbm, grad), (hess_hbm, hess), (margin_hbm, margin)))]
+        (bins_hbm, bins), (node_hbm, node_in), (feat1_hbm, feat1), (bin1_hbm, bin1), (feat2_hbm, feat2), (bin2_hbm, bin2),
+        (grad_hbm, grad), (hess_hbm, hess), (margin_hbm, margin)))]
+    stores = [pltpu.make_async_copy(src, dst, out_sem.at[k]) for k, (src, dst) in enumerate((
+        (out1, out1_hbm), (out2, out2_hbm), (out_margin, margin_out_hbm)))]
     for copy in loads:
         copy.start()
 
@@ -71,36 +76,42 @@
         return pltpu.make_async_remote_copy(
             src_ref=src, dst_ref=dst, send_sem=ss, recv_sem=rs, device_id=peer, device_id_type=MESH)
 
-    line = iota((32, 128), 0)
-    owner = jnp.full((32, 128), -1, jnp.int32)
-    cut = jnp.zeros((32, 128), jnp.int32)
+    for copy in loads[:4]:
+        copy.wait()
+    slot8 = iota((NODES1, 128), 0)
+    low = jnp.full((NODES1, 128), B, jnp.int32)
     for n in range(NODES1):
-        owner = jnp.where(line == n, feat1[n], owner)
-        cut = jnp.where(line == n, bin1[n], cut)
+        at = feat1[n] - feat * features
+        inside = jnp.clip(at, 0, features - 1)
+        first_s[n:n + 1, :] = bins[pl.ds(inside, 1), :]
+        low = jnp.where((slot8 == n) & (jnp.full((NODES1, 128), at, jnp.int32) == inside), bin1[n], low)
+    node_rows = jnp.concatenate([node_in[r:r + 1, :] for r in range(lines)], axis=1)
+    taken = (first_s[...] > low[:, 0:1]) & (node_rows == iota((NODES1, count), 0))
+    x1[3] = jnp.max(jnp.where(taken, 1.0, 0.0), axis=0, keepdims=True)
+    pl.semaphore_wait(barrier, len(peers))
+    route1 = [remote(x1.at[3], x1.at[d - 1], x1_ss.at[d - 1], x1_rs.at[d - 1], across(d)) for d in (1, 2, 3)]
+    for copy in route1:
+        copy.start()
+
+    for copy in loads[4:]:
+        copy.wait()
+    line = iota((NODES2, 128), 0)
+    owner = jnp.full((NODES2, 128), -1, jnp.int32)
+    cut = jnp.zeros((NODES2, 128), jnp.int32)
     for n in range(NODES2):
-        at = 8 + (n % 2) * 8 + n // 2
+        at = (n % 2) * 8 + n // 2
         owner = jnp.where(line == at, feat2[n], owner)
         cut = jnp.where(line == at, bin2[n], cut)
     local = owner - feat * features
-    select = jnp.where(local == iota((32, 128), 1), 1.0, 0.0).astype(bf16)[:, 0:features]
-    for copy in loads:
-        copy.wait()
+    select = jnp.where(local == iota((NODES2, 128), 1), 1.0, 0.0).astype(bf16)[:, 0:features]
     packed[0] = grad[...].astype(f32)
     packed[1] = hess[...].astype(f32)
     packed[2] = node_in[...].astype(f32)
     packed[3] = margin[...]
     values = bins[...].astype(f32)
     picked = lax.dot_general(select, values.astype(bf16), (((1,), (0,)), ((), ())), preferred_element_type=f32)
-    above = jnp.where(picked > cut[:, 0:1].astype(f32), 1.0, 0.0)
+    picked_s[...] = jnp.where(picked > cut[:, 0:1].astype(f32), 1.0, 0.0)
     node = row(2)
-    first = node == iota((NODES1, count), 0).astype(f32)
-    x1[3] = jnp.max(jnp.where(first, above[0:8], 0.0), axis=0, keepdims=True)
-    picked_s[...] = above[8:24]
-    pl.semaphore_wait(barrier, len(peers))
-    route1 = [remote(x1.at[3], x1.at[d - 1], x1_ss.at[d - 1], x1_rs.at[d - 1], across(d)) for d in (1, 2, 3)]
-    for copy in route1:
-        copy.start()
-
     lo = jnp.where(values >= 2.0 * SEG, 2.0, jnp.where(values >= 1.0 * SEG, 1.0, 0.0))
     lo_s[...] = lo
     hi_s[...] = values - SEG * lo
@@ -197,6 +208,7 @@
         result = row(3) + jnp.sum(jnp.where(mine, pick, 0.0), axis=0, keepdims=True)
         for r in range(lines):
             out_margin[r:r + 1, :] = result[:, r * 128:(r + 1) * 128]
+        stores[2].start()
 
     def place(t):
         own, v = t // 9, t % 9
@@ -207,26 +219,26 @@
         j = (1 - own) * (v % 3) + own * (3 - 2 * at2 - late)
         return i, j
 
-    def fill(dst, t, f):
+    def fill(dst, t, f, slot):
         for e in range(2):
-            wide[e, :, 0:LO * COLS] = histogram(f + e)
-        one, two = wide[0], wide[1]
+            wide[slot, e, :, 0:LO * COLS] = histogram(f + e)
+        one, two = wide[slot, 0], wide[slot, 1]
         lane = iota((HI, 128), 1)
         dst[t, 0:HI] = jnp.where(lane < LO * COLS, one, pltpu.roll(two, COLS, 1))
         below = jnp.concatenate([two[FOLD:HI], jnp.zeros((2 * FOLD - HI, 128), f32)], 0)
         dst[t, HI:HI + FOLD] = jnp.where(lane[0:FOLD] < 64, two[0:FOLD], pltpu.roll(below, 64, 1))
 
-    def compute_sent(t, i, j):
-        fill(sent, t, feature(i, j, 1 - c))
-
-    def compute_kept(t, i, j):
-        fill(kept, t, feature(i, j, c))
+    def compute_sent(t, i, j, slot):
+        fill(sent, t, feature(i, j, 1 - c), 2 * slot)
+
+    def compute_kept(t, i, j, slot):
+        fill(kept, t, feature(i, j, c), 2 * slot + 1)
 
     def step(turn, carry):
         for s in range(2):
             t = turn * 2 + s
-            compute_sent(t, *place(t))
-            compute_kept(t, *place(t))
+            compute_sent(t, *place(t), s)
+            compute_kept(t, *place(t), s)
         for s in range(2):
             core_copy(turn * 2 + s).start()
 
@@ -256,17 +268,17 @@
         return carry
 
     lax.fori_loop(0, 7, step, 0)
-    compute_sent(14, 3, 0)
+    compute_sent(14, 3, 0, 0)
     cross_copy().start()
-    compute_kept(14, 3, 0)
+    compute_kept(14, 3, 0, 0)
     p1_copy(14, 11, 0).start()
     finish(13)
     p1_copy(13, 10, 2).start()
     finish(12)
     gather_plane(2)
-    compute_sent(15, 3, 3)
+    compute_sent(15, 3, 3, 1)
     core_copy(15).start()
-    compute_kept(15, 3, 3)
+    compute_kept(15, 3, 3, 1)
     leaves_3()
     finish(15)
     for i in range(3):
@@ -308,6 +320,8 @@
                 for n in range(NODES1):
                     out[n * stride + side, e:e + 1, :] = gain[side * 8 + n:side * 8 + n + 1]
 
+    for copy in stores[:2]:
+        copy.start()
     for copy in route1 + route2 + leaf_copy(0) + leaf_copy(1) + leaf_copy(2):
         copy.wait_send()
     for t in list(range(14)) + [15]:
@@ -319,6 +333,8 @@
     cross_copy().wait_send()
     for i in range(3):
         p2_copy(i).wait_send()
+    for copy in stores:
+        copy.wait()
 
 
 def copy_kernel(a, b, d, a_out, b_out, d_out):
@@ -348,16 +364,24 @@
             jax.ShapeDtypeStruct((NODES1, own, B), f32),
             jax.ShapeDtypeStruct((NODES2, own, B), f32),
             jax.ShapeDtypeStruct(lines, f32)),
-        in_specs=[pl.BlockSpec(memory_space=pltpu.HBM)] * 5 + [pl.BlockSpec(memory_space=pltpu.SMEM)] * 4,
-        out_specs=[pl.BlockSpec(memory_space=pltpu.VMEM)] * 3,
+        in_specs=[pl.BlockSpec(memory_space=pltpu.HBM)] * 9,
+        out_specs=[pl.BlockSpec(memory_space=pltpu.HBM)] * 3,
         scratch_shapes=[
             pltpu.VMEM((features, count), jnp.int32),
             pltpu.VMEM(lines, bf16),
             pltpu.VMEM(lines, bf16),
             pltpu.VMEM(lines, f32),
             pltpu.VMEM(lines, jnp.int32),
+            pltpu.SMEM((NODES1,), jnp.int32),
+            pltpu.SMEM((NODES1,), jnp.int32),
+            pltpu.SMEM((NODES2,), jnp.int32),
+            pltpu.SMEM((NODES2,), jnp.int32),
+            pltpu.VMEM((NODES1, own, B), f32),
+            pltpu.VMEM((NODES2, own, B), f32),
+            pltpu.VMEM(lines, f32),
             pltpu.VMEM((4,) + lines, f32),
-            dma((5,)),
+            pltpu.VMEM((NODES1, count), jnp.int32),
+            dma((9,)), dma((3,)),
             pltpu.VMEM((features, count), f32),
             pltpu.VMEM((features, count), f32),
             pltpu.VMEM((COLS, count), bf16),
@@ -375,7 +399,7 @@
             pltpu.VMEM((COLS, 128), f32),
             pltpu.VMEM((3, COLS, 128), f32),
             pltpu.VMEM((3, COLS, 128), f32),
-            pltpu.VMEM((2, HI, 128), f32),
+            pltpu.VMEM((4, 2, HI, 128), f32),
             dma((3,)), dma((3,)), dma((3,)), dma((3,)),
             dma((16,)), dma((16,)), dma((13,)), dma((13,)), dma((3,)), dma((3,)),
             dma((7,)), dma((7,)),

time: 36.6 us -> 35.9 us (0.981)
  Pallas kernels: 35.7 us -> 35 us
    pallas_call x1, Pallas kernels: 34.3 us -> 33.6 us  [body(): pl.pallas_call(kernel, out_shape=(jax.ShapeDtypeStruct((NODES1, own, B),...]
where the time goes in v4:
time: 35.9 us; the launch traced here: 35.7 us
  Pallas kernels  35 us (97%)
  between operations  0.64 us (2%)
    pallas_call x1, Pallas kernels, body(): pl.pallas_call(kernel, out_shape=(jax.ShapeDtypeStruct((NODES1, own, B),...  33.6 us
    pallas_call x1, Pallas kernels, hand_out(): pl.pallas_call(copy_kernel, out_shape=tuple((jax.ShapeDtypeStruct(a.shape...  1.39 us

profile of v4, /device:TPU:1, one launch (start us, length us, event | category | flops | bytes accessed | tf_op | source)
XLA Modules:
  0.0 35.7 jit_solution(12562488540866738225)
XLA Ops:
  0.6 33.6 %shard_map.112 = (f32[8,2,256]{2,1,0:T(2,128)}, f32[16,2,256]{2,1,0:T(2,128)}, f32[32,128]{1,0:T(8,128)}) custom-call(s32[64,4096]{1,0:T(8,128)} %bins_hbm.1, bf16[32,128]{1,0:T(8,128)(2,1)} %bitcast.8, bf16[32,128]{1,0:T(8,128)(2,1)} %bitcast.9, f32[32,128]{1,0:T(8,128)} %bitcast.5, s32[32,128]{1,0:T(8,128)} %bitcast.6, s32[8]{0:T(128)} %feat1_hbm.1, ...), custom_call_target="tpu_custom_call" | custom-call | flops 4294967296 | bytes 1048576 | tf_op jit(solution)/shard_map/pallas_call | solution.py:361
  34.3 1.4 %hand_out.1 = (f32[8,2,256]{2,1,0:T(2,128)}, f32[16,2,256]{2,1,0:T(2,128)}, f32[32,128]{1,0:T(8,128)}) custom-call(f32[8,2,256]{2,1,0:T(2,128)} %get-tuple-element.9.a, f32[16,2,256]{2,1,0:T(2,128)} %get-tuple-element.10.b, f32[32,128]{1,0:T(8,128)} %get-tuple-element.11.d), custom_call_target="tpu_custom_call" | custom-call | tf_op jit(solution)/shard_map/hand_out/pallas_call | solution.py:346

commit v5 on v4

--- a/solution.py
+++ b/solution.py
@@ -272,12 +272,12 @@
     cross_copy().start()
     compute_kept(14, 3, 0, 0)
     p1_copy(14, 11, 0).start()
+    compute_sent(15, 3, 3, 1)
+    core_copy(15).start()
     finish(13)
     p1_copy(13, 10, 2).start()
     finish(12)
     gather_plane(2)
-    compute_sent(15, 3, 3, 1)
-    core_copy(15).start()
     compute_kept(15, 3, 3, 1)
     leaves_3()
     finish(15)

time: 35.9 us -> 35.9 us (level)
  no operation moved by 1% of the time
where the time goes in v5:
time: 35.9 us; the launch traced here: 35.7 us
  Pallas kernels  35 us (97%)
  between operations  0.64 us (2%)
    pallas_call x1, Pallas kernels, body(): pl.pallas_call(kernel, out_shape=(jax.ShapeDtypeStruct((NODES1, own, B),...  33.6 us
    pallas_call x1, Pallas kernels, hand_out(): pl.pallas_call(copy_kernel, out_shape=tuple((jax.ShapeDtypeStruct(a.shape...  1.39 us

profile of v5, /device:TPU:1, one launch (start us, length us, event | category | flops | bytes accessed | tf_op | source)
XLA Modules:
  0.0 35.7 jit_solution(15862559023453615634)
XLA Ops:
  0.6 33.6 %shard_map.112 = (f32[8,2,256]{2,1,0:T(2,128)}, f32[16,2,256]{2,1,0:T(2,128)}, f32[32,128]{1,0:T(8,128)}) custom-call(s32[64,4096]{1,0:T(8,128)} %bins_hbm.1, bf16[32,128]{1,0:T(8,128)(2,1)} %bitcast.8, bf16[32,128]{1,0:T(8,128)(2,1)} %bitcast.9, f32[32,128]{1,0:T(8,128)} %bitcast.5, s32[32,128]{1,0:T(8,128)} %bitcast.6, s32[8]{0:T(128)} %feat1_hbm.1, ...), custom_call_target="tpu_custom_call" | custom-call | flops 4294967296 | bytes 1048576 | tf_op jit(solution)/shard_map/pallas_call | solution.py:361
  34.3 1.4 %hand_out.1 = (f32[8,2,256]{2,1,0:T(2,128)}, f32[16,2,256]{2,1,0:T(2,128)}, f32[32,128]{1,0:T(8,128)}) custom-call(f32[8,2,256]{2,1,0:T(2,128)} %get-tuple-element.9.a, f32[16,2,256]{2,1,0:T(2,128)} %get-tuple-element.10.b, f32[32,128]{1,0:T(8,128)} %get-tuple-element.11.d), custom_call_target="tpu_custom_call" | custom-call | tf_op jit(solution)/shard_map/hand_out/pallas_call | solution.py:346

commit v6 on v5

--- a/solution.py
+++ b/solution.py
@@ -280,14 +280,15 @@
     gather_plane(2)
     compute_kept(15, 3, 3, 1)
     leaves_3()
-    finish(15)
     for i in range(3):
         p2_copy(i).wait_recv()
     for t, slot, j in ((11, 9, 1), (13, 10, 2), (14, 11, 0)):
         p1_copy(t, slot, j).wait_recv()
     cross_copy().wait_recv()
 
-    hist = (kept[15] + part2[0] + part2[1] + part2[2] + part1[9] + part1[10] + part1[11] + part1[12])
+    hist = kept[15] + part2[0] + part2[1] + part2[2] + part1[9] + part1[10] + part1[11] + part1[12]
+    core_copy(15).wait_recv()
+    hist += mate[15]
 
     def split(x):
         a = x.astype(bf16)

time: 35.9 us -> 35.9 us (level)
  no operation moved by 1% of the time
where the time goes in v6:
time: 35.9 us; the launch traced here: 35.7 us
  Pallas kernels  35 us (97%)
  between operations  0.64 us (2%)
    pallas_call x1, Pallas kernels, body(): pl.pallas_call(kernel, out_shape=(jax.ShapeDtypeStruct((NODES1, own, B),...  33.6 us
    pallas_call x1, Pallas kernels, hand_out(): pl.pallas_call(copy_kernel, out_shape=tuple((jax.ShapeDtypeStruct(a.shape...  1.39 us

profile of v6, /device:TPU:1, one launch (start us, length us, event | category | flops | bytes accessed | tf_op | source)
XLA Modules:
  0.0 35.7 jit_solution(11372590026635461616)
XLA Ops:
  0.6 33.6 %shard_map.112 = (f32[8,2,256]{2,1,0:T(2,128)}, f32[16,2,256]{2,1,0:T(2,128)}, f32[32,128]{1,0:T(8,128)}) custom-call(s32[64,4096]{1,0:T(8,128)} %bins_hbm.1, bf16[32,128]{1,0:T(8,128)(2,1)} %bitcast.8, bf16[32,128]{1,0:T(8,128)(2,1)} %bitcast.9, f32[32,128]{1,0:T(8,128)} %bitcast.5, s32[32,128]{1,0:T(8,128)} %bitcast.6, s32[8]{0:T(128)} %feat1_hbm.1, ...), custom_call_target="tpu_custom_call" | custom-call | flops 4294967296 | bytes 1048576 | tf_op jit(solution)/shard_map/pallas_call | solution.py:362
  34.3 1.4 %hand_out.1 = (f32[8,2,256]{2,1,0:T(2,128)}, f32[16,2,256]{2,1,0:T(2,128)}, f32[32,128]{1,0:T(8,128)}) custom-call(f32[8,2,256]{2,1,0:T(2,128)} %get-tuple-element.9.a, f32[16,2,256]{2,1,0:T(2,128)} %get-tuple-element.10.b, f32[32,128]{1,0:T(8,128)} %get-tuple-element.11.d), custom_call_target="tpu_custom_call" | custom-call | tf_op jit(solution)/shard_map/hand_out/pallas_call | solution.py:347
